TPU v7x, 32 devices: a whole 2x2x4 slice. The times are simulated.
32 devices in a mesh: lat: 8 (over z, x), lon: 4 (over y, core).
Axes of the slice: x: 2, y: 2, z: 4, core: 2. Of those that a mesh axis runs over, the one named last changes fastest.
Arguments:
- tangent: float32 [256, 3, 32, 512], P(None, None, 'lat', 'lon'), may hold values from -40 to 40
- base_state: float32 [4, 32, 512], P(None, 'lat', 'lon'), may hold values from -0.4 to 0.8
Outputs:
- fields: float32 [256, 3, 32, 512], P(None, None, 'lat', 'lon')
- upper: float32 [256, 256], replicated
All inputs are finite; a program needn't handle non-finite values.
Results may differ from a plain program's by a relative error of at most 0.00012.
Values sent between devices are 32-bit elements; how exact they have to be, the bound alone decides.
A program may use at most 64 MiB of HBM per device.

v0:
```python
import jax
import jax.numpy as jnp
from jax import lax
from jax.sharding import PartitionSpec as P

gravity_coef = 0.5


def with_halo(shard, sides, width, wrap):
    for axis, dim in sides:
        peers, length = (lax.axis_size(axis), shard.shape[dim])
        up = [(i, (i + 1) % peers) for i in range(peers if wrap else peers - 1)]
        down = [(j, i) for i, j in up]
        last = lax.slice_in_dim(shard, length - width, length, axis=dim)
        first = lax.slice_in_dim(shard, 0, width, axis=dim)
        before = lax.ppermute(last, axis, up)
        after = lax.ppermute(first, axis, down)
        shard = jnp.concatenate([before, shard, after], axis=dim)
    return shard


def east_west(field):
    return 0.5 * (field[..., 1:-1, 2:] - field[..., 1:-1, :-2])


def north_south(field):
    return 0.5 * (field[..., 2:, 1:-1] - field[..., :-2, 1:-1])


def advance(padded, coefficients):
    thickness = padded[:, 0]
    zonal = padded[:, 1]
    meridional = padded[:, 2]
    centre = padded[:, :, 1:-1, 1:-1]
    drift_x = coefficients[0]
    drift_y = coefficients[1]
    depth_field = coefficients[2]
    rotation = coefficients[3]

    def carried(field):
        return drift_x * east_west(field) + drift_y * north_south(field)

    new_thick = (
        centre[:, 0]
        - carried(thickness)
        - depth_field * (east_west(zonal) + north_south(meridional))
    )
    new_zonal = (
        centre[:, 1]
        - carried(zonal)
        + rotation * centre[:, 2]
        - gravity_coef * east_west(thickness)
    )
    new_merid = (
        centre[:, 2]
        - carried(meridional)
        - rotation * centre[:, 1]
        - gravity_coef * north_south(thickness)
    )
    return jnp.stack([new_thick, new_zonal, new_merid], axis=1)


def per_device(tangent, base_state):
    lat_count = lax.axis_size("lat")
    lon_count = lax.axis_size("lon")
    vectors = tangent.shape[0]
    lat_cells = tangent.shape[2]
    lon_cells = tangent.shape[3]
    padded = with_halo(tangent, (("lon", 3),), 2, True)
    padded = with_halo(padded, (("lat", 2),), 2, False)
    beside_all = with_halo(base_state, (("lon", 2),), 1, True)
    beside_all = with_halo(beside_all, (("lat", 1),), 1, False)
    first = advance(padded, beside_all)
    row_index = lax.axis_index("lat") * lat_cells - 1 + jnp.arange(lat_cells + 2, dtype=jnp.int32)
    inside = (row_index >= 0) & (row_index < lat_cells * lat_count)
    first = jnp.where(inside[:, None], first, jnp.float32(0.0))
    state = advance(first, base_state)
    flat = state.reshape(vectors, -1)
    cell_total = lat_cells * lon_cells * lat_count * lon_count
    local_gram = jnp.dot(
        flat, flat.T, precision=lax.Precision.HIGHEST, preferred_element_type=jnp.float32
    )
    total = lax.psum(local_gram, ("lat", "lon"))
    lower_factor = jnp.linalg.cholesky(total / cell_total)
    fields = lax.linalg.triangular_solve(lower_factor, flat, left_side=True, lower=True)
    return (fields.reshape(state.shape), lower_factor.T)


def solution(mesh):
    in_specs = (P(None, None, "lat", "lon"), P(None, "lat", "lon"))
    out_specs = (P(None, None, "lat", "lon"), P())
    return jax.shard_map(
        per_device, mesh=mesh, in_specs=in_specs, out_specs=out_specs, check_vma=False
    )
```

profile of v0, /device:TPU:0, one launch (start us, length us, event | category | flops | bytes accessed | tf_op | source)
XLA Modules:
  0.0 290.8 jit_solution(12232453055552341266)
XLA Ops:
  7.2 0.0 all-reduce.3.cloned.1.call-start
  7.2 4.2 %fusion.45 = (f32[256,3,4,2]{3,2,1,0:T(4,128)S(1)}, f32[256,3,4,2]{3,2,1,0:T(4,128)}) fusion(f32[256,3,4,128]{3,2,1,0:T(4,128)} %param.2), kind=kLoop, calls=%fused_computation.108 | loop fusion | bytes 98304 | tf_op jit(solution)/shard_map/slice | solution.py:14
  11.4 1.8 copy.36
  13.1 2.5 collective-permute-start.1
  15.6 0.6 copy.35
  16.2 0.1 collective-permute-start
  16.3 0.1 fusion.46
  16.4 1.7 collective-permute-start.5
  18.1 0.1 copy.21
  18.3 0.5 copy.22
  18.8 0.8 collective-permute-done
  19.5 1.7 copy.20
  21.2 2.7 pad_maximum_fusion.1
  23.9 1.9 fusion.43
  25.8 2.5 copy.24
  28.3 1.3 collective-permute-start.3
  29.6 2.5 copy.23
  32.1 5.5 %collective-permute-start.2 = (f32[256,3,2,132]{0,2,3,1:T(2,128)}, f32[256,3,2,132]{0,2,3,1:T(2,128)}, u32[]{:S(2)}, u32[]{:S(2)}) collective-permute-start(f32[256,3,2,132]{0,2,3,1:T(2,128)} %copy.23), channel_id=1, source_target_pairs={{0,4},{4,8},{8,12},{12,16},{16,20},{20,24},{24,28},{1,5},{5,9},{9,... | collective-permute-start | bytes 2433032 | tf_op jit(solution)/shard_map/ppermute | solution.py:16
  37.5 0.1 pad_maximum_fusion.7
  37.6 1.3 collective-permute-start.7
  38.9 4.5 %collective-permute-start.6 = (f32[4,1,130]{2,1,0:T(1,128)S(1)}, f32[4,1,130]{2,1,0:T(1,128)S(1)}, u32[]{:S(2)}, u32[]{:S(2)}) collective-permute-start(f32[4,1,130]{2,1,0:T(1,128)S(1)} %get-tuple-element.52), channel_id=1, source_target_pairs={{0,4},{4,8},{8,12},{12,16},{16,20},{20,24},{24,28},{1,5},{5,9},{9,... | collective-permute-start | bytes 6248 | tf_op jit(solution)/shard_map/ppermute | solution.py:16
  43.5 6.9 %collective-permute-done.7 = f32[4,1,130]{2,1,0:T(1,128)S(1)} collective-permute-done((f32[4,1,130]{2,1,0:T(1,128)S(1)}, f32[4,1,130]{2,1,0:T(1,128)S(1)}, u32[]{:S(2)}, u32[]{:S(2)}) %collective-permute-start.7) | collective-permute-done | bytes 2112 | tf_op jit(solution)/shard_map/ppermute | solution.py:17
  50.4 17.4 %collective-permute-done.6 = f32[4,1,130]{2,1,0:T(1,128)S(1)} collective-permute-done((f32[4,1,130]{2,1,0:T(1,128)S(1)}, f32[4,1,130]{2,1,0:T(1,128)S(1)}, u32[]{:S(2)}, u32[]{:S(2)}) %collective-permute-start.6) | collective-permute-done | bytes 2112 | tf_op jit(solution)/shard_map/ppermute | solution.py:16
  67.8 0.1 pad_maximum_fusion.4
  67.9 2.5 copy.26
  70.4 2.5 copy.25
  72.9 3.6 %pad_maximum_fusion = f32[256,3,8,132]{3,0,2,1:T(8,128)S(1)} fusion(f32[256,3,2,132]{3,0,2,1:T(8,128)} %copy.26, f32[256,3,4,2]{3,0,2,1:T(8,128)S(1)} %copy.22, f32[256,3,4,128]{3,0,2,1:T(8,128)S(1)} %copy.21, f32[256,3,4,2]{3,0,2,1:T(8,128)} %copy.20, f32[256,3,2,132]{3,0,2,1:T(8,128)} %copy.25), kind=kLoop, calls=%fused_computation.2 | loop fusion | flops 3244032 | bytes 6488064 | tf_op jit(solution)/shard_map/concatenate | solution.py:18
  76.5 0.6 slice_bitcast_fusion.1
  77.1 4.8 %fusion.11 = (f32[256,1,6,130]{3,0,2,1:T(8,128)S(1)}, f32[256,1,6,130]{3,0,2,1:T(8,128)S(1)}) fusion(f32[256,8,132]{2,0,1:T(8,128)S(1)} %get-tuple-element.30, f32[256,3,8,132]{3,0,2,1:T(8,128)S(1)} %pad_maximum_fusion, f32[6,130]{1,0:T(8,128)S(1)} %get-tuple-element.49, f32[6,130]{1,0:T(8,128)S(1)} %get-tuple-element.50, ...), kind=kLoop, calls=%fused_computation.26 | loop fusion | flops 4392960 | bytes 12788880 | tf_op jit(solution)/shard_map/stack | solution.py:60
  82.0 2.9 %fusion.14 = f32[256,1,6,130]{3,0,2,1:T(8,128)S(1)} fusion(f32[256,3,8,132]{3,0,2,1:T(8,128)S(1)} %pad_maximum_fusion, f32[6,130]{1,0:T(8,128)S(1)} %get-tuple-element.48, f32[6,130]{1,0:T(8,128)S(1)} %get-tuple-element.50, f32[6,130]{1,0:T(8,128)S(1)} %get-tuple-element.51, f32[256,8,132]{2,0,1:T(8,128)S(1)} %get-tuple-element.32, ...), kind=kLoop, calls=%fused_computation.35 | loop fusion | flops 2196480 | bytes 7996560 | tf_op jit(solution)/shard_map/stack | solution.py:60
  84.9 0.5 maximum_select_fusion
  85.4 0.4 slice_bitcast_fusion.4
  85.9 1.6 fusion.26
  87.4 1.0 fusion.29
  88.4 0.1 pad_maximum_fusion.2
  88.6 2.1 convolution_bitcast_fusion
  90.7 0.0 all-reduce.3.cloned.1.call-update
  90.8 0.1 fusion.44
  90.9 0.3 copy.30
  91.2 0.3 copy.31
  91.5 0.3 copy.29
  91.7 125.3 %all-reduce.3.cloned.1.call-done = f32[256,256]{0,1:T(8,128)} async-done(((f32[256,256]{0,1:T(8,128)}), f32[256,256]{0,1:T(8,128)}) %all-reduce.3.cloned.1.call-update) | async-done | bytes 262160 | tf_op jit(solution)/shard_map/psum | solution.py:83
  217.0 1.0 broadcast_multiply_fusion
  218.0 0.1 copy.28
  218.1 1.0 fusion.30
  219.1 11.8 %cholesky.50 = f32[128,128]{1,0:T(8,128)S(1)} custom-call(f32[128,128]{1,0:T(8,128)S(1)} %cholesky.118), custom_call_target="Cholesky" | custom-call | tf_op jit(solution)/shard_map/jit(cholesky)/cholesky | solution.py:84
  231.0 9.8 %custom-call.14 = f32[1,128,128]{1,2,0:T(8,128)S(1)} custom-call(f32[1,128,128]{2,1,0:T(8,128)S(1)} %get-tuple-element.47), custom_call_target="InvertDiagBlocksLowerTriangular" | custom-call | tf_op jit(solution)/shard_map/jit(cholesky)/cholesky | solution.py:84
  240.8 0.2 constant_dynamic-update-slice_fusion.1
  241.1 0.3 convolution_subtract_fusion.1
  241.3 11.7 %cholesky.105 = f32[128,128]{1,0:T(8,128)S(1)} custom-call(f32[128,128]{1,0:T(8,128)S(1)} %convolution_subtract_fusion.1), custom_call_target="Cholesky" | custom-call | tf_op jit(solution)/shard_map/jit(cholesky)/cholesky | solution.py:84
  253.1 0.6 compare_reduce_fusion
  255.1 0.1 triangular_solve.61
  255.1 4.0 %while.1 = (s32[]{:T(128)}, f32[256,256]{1,0:T(8,128)S(1)}, s32[2,2]{1,0:T(2,128)S(1)}, f32[2,128,128]{2,1,0:T(8,128)S(1)}, s32[]{:T(128)}) while((s32[]{:T(128)}, f32[256,256]{1,0:T(8,128)S(1)}, s32[2,2]{1,0:T(2,128)S(1)}, f32[2,128,128]{2,1,0:T(8,128)S(1)}, s32[]{:T(128)}) %tuple.48), condition=%wide.while_cond, body=%wide.while_body.sunk | while | flops 2 | bytes 131189 | solution.py:85
  255.1 0.6 fusion.53
  255.7 1.4 bitcast_dynamic-update-slice_fusion.2
  257.1 0.6 fusion.53
  257.7 1.4 bitcast_dynamic-update-slice_fusion.2
  259.1 19.7 %custom-call.15 = f32[2,128,128]{1,2,0:T(8,128)S(1)} custom-call(f32[2,128,128]{2,1,0:T(8,128)S(1)} %get-tuple-element.9), custom_call_target="InvertDiagBlocksLowerTriangular" | custom-call | tf_op jit(solution)/shard_map/triangular_solve | solution.py:85
  278.8 0.9 fusion.35
  279.7 0.8 convolution_subtract_fusion
  280.5 0.8 fusion.34
  281.3 0.1 pad_maximum_fusion.3
  281.4 1.6 reshape.39
  283.1 0.8 copy.32
  (22 shorter events, 0.2 us)
Async XLA Ops:
  7.2 209.8 %all-reduce.3.cloned.1.call-start = ((), (), s32[]{:S(2)}) async-start(), calls=%async_computation | async-start | bytes 524288 | tf_op jit(solution)/shard_map/psum | solution.py:83
  11.4 4.9 %copy-start.1 = (f32[4,4,128]{2,1,0:T(4,128)S(1)}, f32[4,4,128]{2,1,0:T(4,128)}, u32[]{:S(2)}) copy-start(f32[4,4,128]{2,1,0:T(4,128)} %param.3) | copy-start | bytes 24580
  11.4 6.7 %copy-start = (f32[256,3,4,128]{3,2,1,0:T(4,128)S(1)}, f32[256,3,4,128]{3,2,1,0:T(4,128)}, u32[]{:S(2)}) copy-start(f32[256,3,4,128]{3,2,1,0:T(4,128)} %param.2) | copy-start | bytes 4718596
  13.1 5.1 %collective-permute-start.1 = (f32[256,3,4,2]{0,2,3,1:T(4,128)S(1)}, f32[256,3,4,2]{0,2,3,1:T(4,128)S(1)}, u32[]{:S(2)}, u32[]{:S(2)}) collective-permute-start(f32[256,3,4,2]{0,2,3,1:T(4,128)S(1)} %copy.36), channel_id=1, source_target_pairs={{1,0},{2,1},{3,2},{0,3},{5,4},{6,5},{7,6},{4,7},{9,8},{10,9},{11,1... | collective-permute-start | bytes 73736 | tf_op jit(solution)/shard_map/ppermute | solution.py:17
  16.2 3.3 %collective-permute-start = (f32[256,3,4,2]{0,2,3,1:T(4,128)S(1)}, f32[256,3,4,2]{0,2,3,1:T(4,128)S(1)}, u32[]{:S(2)}, u32[]{:S(2)}) collective-permute-start(f32[256,3,4,2]{0,2,3,1:T(4,128)S(1)} %copy.35), channel_id=1, source_target_pairs={{0,1},{1,2},{2,3},{3,0},{4,5},{5,6},{6,7},{7,4},{8,9},{9,10},{10,1... | collective-permute-start | bytes 73736 | tf_op jit(solution)/shard_map/ppermute | solution.py:16
  16.4 21.1 %collective-permute-start.5 = (f32[4,4,1]{2,1,0:T(4,128)S(1)}, f32[4,4,1]{2,1,0:T(4,128)S(1)}, u32[]{:S(2)}, u32[]{:S(2)}) collective-permute-start(f32[4,4,1]{2,1,0:T(4,128)S(1)} %get-tuple-element.59), channel_id=1, source_target_pairs={{1,0},{2,1},{3,2},{0,3},{5,4},{6,5},{7,6},{4,7},{9,8},{10,9},{11,1... | collective-permute-start | bytes 200 | tf_op jit(solution)/shard_map/ppermute | solution.py:17
  18.1 19.4 %collective-permute-start.4 = (f32[4,4,1]{2,1,0:T(4,128)S(1)}, f32[4,4,1]{2,1,0:T(4,128)S(1)}, u32[]{:S(2)}, u32[]{:S(2)}) collective-permute-start(f32[4,4,1]{2,1,0:T(4,128)S(1)} %get-tuple-element.58), channel_id=1, source_target_pairs={{0,1},{1,2},{2,3},{3,0},{4,5},{5,6},{6,7},{7,4},{8,9},{9,10},{10,1... | collective-permute-start | bytes 200 | tf_op jit(solution)/shard_map/ppermute | solution.py:16
  28.3 39.6 %collective-permute-start.3 = (f32[256,3,2,132]{0,2,3,1:T(2,128)}, f32[256,3,2,132]{0,2,3,1:T(2,128)}, u32[]{:S(2)}, u32[]{:S(2)}) collective-permute-start(f32[256,3,2,132]{0,2,3,1:T(2,128)} %copy.24), channel_id=1, source_target_pairs={{4,0},{8,4},{12,8},{16,12},{20,16},{24,20},{28,24},{5,1},{9,5},{13... | collective-permute-start | bytes 2433032 | tf_op jit(solution)/shard_map/ppermute | solution.py:17
  32.1 38.3 %collective-permute-start.2 = (f32[256,3,2,132]{0,2,3,1:T(2,128)}, f32[256,3,2,132]{0,2,3,1:T(2,128)}, u32[]{:S(2)}, u32[]{:S(2)}) collective-permute-start(f32[256,3,2,132]{0,2,3,1:T(2,128)} %copy.23), channel_id=1, source_target_pairs={{0,4},{4,8},{8,12},{12,16},{16,20},{20,24},{24,28},{1,5},{5,9},{9,... | collective-permute-start | bytes 2433032 | tf_op jit(solution)/shard_map/ppermute | solution.py:16
  37.6 12.8 %collective-permute-start.7 = (f32[4,1,130]{2,1,0:T(1,128)S(1)}, f32[4,1,130]{2,1,0:T(1,128)S(1)}, u32[]{:S(2)}, u32[]{:S(2)}) collective-permute-start(f32[4,1,130]{2,1,0:T(1,128)S(1)} %get-tuple-element.53), channel_id=1, source_target_pairs={{4,0},{8,4},{12,8},{16,12},{20,16},{24,20},{28,24},{5,1},{9,5},{13... | collective-permute-start | bytes 6248 | tf_op jit(solution)/shard_map/ppermute | solution.py:17
  38.9 28.9 %collective-permute-start.6 = (f32[4,1,130]{2,1,0:T(1,128)S(1)}, f32[4,1,130]{2,1,0:T(1,128)S(1)}, u32[]{:S(2)}, u32[]{:S(2)}) collective-permute-start(f32[4,1,130]{2,1,0:T(1,128)S(1)} %get-tuple-element.52), channel_id=1, source_target_pairs={{0,4},{4,8},{8,12},{12,16},{16,20},{20,24},{24,28},{1,5},{5,9},{9,... | collective-permute-start | bytes 6248 | tf_op jit(solution)/shard_map/ppermute | solution.py:16
Sparse Core Ops, SparseCore 0:
  90.9 126.0 all-reduce.2
where the time goes:
time: 291 us
  waiting for transfers between devices  150 us (52%)
  other arithmetic  73.4 us (25%)
  local copies, waits for them, and re-layouts  29.4 us (10%)
  starting transfers between devices  16.9 us (6%)
  between operations  15.6 us (5%)
  matrix products  5.12 us (2%)
    psum x1, waiting for transfers between devices, per_device(): total = lax.psum(local_gram, ('lat', 'lon'))  125 us
    another operation x6, other arithmetic, per_device(): lower_factor = jnp.linalg.cholesky(total / cell_total)  34.1 us
    another operation x3, other arithmetic, per_device(): lax.linalg.triangular_solve(lower_factor, flat, left_side=True, lower=True)  19.8 us
    ppermute x4, waiting for transfers between devices, with_halo(): before = lax.ppermute(last, axis, up)  18.1 us
    another operation x5, other arithmetic, advance(): return jnp.stack([new_thick, new_zonal, new_merid], axis=1)  10.5 us
    ppermute x4, starting transfers between devices, with_halo(): before = lax.ppermute(last, axis, up)  10.1 us
    slice x4, local copies, waits for them, and re-layouts, with_halo(): last = lax.slice_in_dim(shard, length - width, length, axis=dim)  8.61 us
    ppermute x4, waiting for transfers between devices, with_halo(): after = lax.ppermute(first, axis, down)  6.93 us
  transfers between devices with their start and end apart: 9, of which 4 were waited for; matrix products, arithmetic and copies ran while one was open for 6% of the time, Pallas kernels for 0%

commit v1 on v0

v1 whole, which is shorter than its diff:
```python
import functools

import jax
import jax.numpy as jnp
from jax import lax
from jax.experimental import pallas as pl
from jax.experimental.pallas import tpu as pltpu
from jax.sharding import PartitionSpec as P

MESH = pl.DeviceIdType.MESH
HIGHEST = lax.Precision.HIGHEST
GRAVITY = 0.5
CHUNKS = 4
BLOCK = 32


def dot_t(a, b):
    return lax.dot_general(
        a, b, (((1,), (1,)), ((), ())), precision=HIGHEST, preferred_element_type=jnp.float32
    )


def t_dot(a, b):
    return lax.dot_general(
        a, b, (((0,), (0,)), ((), ())), precision=HIGHEST, preferred_element_type=jnp.float32
    )


def dot(a, b):
    return jnp.dot(a, b, precision=HIGHEST, preferred_element_type=jnp.float32)


def step_kernel(
    lat_n, lon_n, rows, vectors, fused, x_ref, base_ref, s_ref, gram_ref,
    state, above, below, to_west, to_east, from_west, from_east,
    gram, lon_buf, lat_buf, part, piece, gathered,
    row_send, row_recv, col_send, col_recv,
    rs_lon_send, rs_lon_recv, rs_lat_send, rs_lat_recv,
    ag_lat_send, ag_lat_recv, ag_lon_send, ag_lon_recv,
):
    lat = lax.axis_index("lat")
    lon = lax.axis_index("lon")
    cells = x_ref.shape[1]
    size = vectors // CHUNKS
    planes = 3 * rows

    def lon_peer(d):
        return lax.rem(lon + d, lon_n)

    def lat_peer(d):
        return lax.rem(lat + d, lat_n)

    barrier = pltpu.get_barrier_semaphore()
    for d in range(1, lon_n):
        pl.semaphore_signal(barrier, inc=1, device_id=(lat, lon_peer(d)), device_id_type=MESH)
    for d in range(1, lat_n):
        pl.semaphore_signal(barrier, inc=1, device_id=(lat_peer(d), lon), device_id_type=MESH)
    pl.semaphore_wait(barrier, lon_n + lat_n - 2)

    lane = lax.broadcasted_iota(jnp.int32, (size, cells), 1)

    def span(c):
        return pl.ds(c * size, size)

    def row_copy(phase, c, up):
        src = rows - 1 if up else 0
        dst = above if up else below
        side = 0 if up else 1
        peer = lat + 1 if up else lat - 1
        return pltpu.make_async_remote_copy(
            src_ref=state.at[phase, src, :, span(c), :],
            dst_ref=dst.at[phase, :, span(c), :],
            send_sem=row_send.at[phase, c, side],
            recv_sem=row_recv.at[phase, c, side],
            device_id=(peer, lon),
            device_id_type=MESH,
        )

    def col_copy(phase, c, east):
        side = 0 if east else 1
        return pltpu.make_async_remote_copy(
            src_ref=(to_east if east else to_west).at[phase, span(c), :],
            dst_ref=(from_west if east else from_east).at[phase, span(c), :],
            send_sem=col_send.at[phase, c, side],
            recv_sem=col_recv.at[phase, c, side],
            device_id=(lat, lon_peer(1) if east else lon_peer(lon_n - 1)),
            device_id_type=MESH,
        )

    def send(phase, c):
        @pl.when(lat < lat_n - 1)
        def _():
            row_copy(phase, c, True).start()

        @pl.when(lat > 0)
        def _():
            row_copy(phase, c, False).start()

        col_copy(phase, c, True).start()
        col_copy(phase, c, False).start()

    def pack(phase, c):
        west = jnp.zeros((size, cells), jnp.float32)
        east = jnp.zeros((size, cells), jnp.float32)
        for r in range(rows):
            for f in range(3):
                p = f * rows + r
                q = state[phase, r, f, span(c), :]
                west = jnp.where(lane == p, pltpu.roll(q, p, 1) if p else q, west)
                east = jnp.where(lane == p, pltpu.roll(q, p + 1, 1), east)
        to_west[phase, span(c), :] = west
        to_east[phase, span(c), :] = east

    def receive(phase, c):
        @pl.when(lat > 0)
        def _():
            row_copy(phase, c, True).wait_recv()

        @pl.when(lat < lat_n - 1)
        def _():
            row_copy(phase, c, False).wait_recv()

        col_copy(phase, c, True).wait_recv()
        col_copy(phase, c, False).wait_recv()

    def sent(phase, c):
        @pl.when(lat < lat_n - 1)
        def _():
            row_copy(phase, c, True).wait_send()

        @pl.when(lat > 0)
        def _():
            row_copy(phase, c, False).wait_send()

        col_copy(phase, c, True).wait_send()
        col_copy(phase, c, False).wait_send()

    def field(phase, r, f, c):
        if r < 0:
            return above[phase, f, span(c), :]
        if r >= rows:
            return below[phase, f, span(c), :]
        return state[phase, r, f, span(c), :]

    def advance(phase, c):
        west_in = from_west[phase, span(c), :]
        east_in = from_east[phase, span(c), :]

        def across(q, p):
            west = jnp.where(lane == 0, pltpu.roll(west_in, cells - p, 1) if p else west_in, pltpu.roll(q, 1, 1))
            east = jnp.where(lane == cells - 1, pltpu.roll(east_in, cells - 1 - p, 1), pltpu.roll(q, cells - 1, 1))
            return east - west

        for r in range(rows):
            half_x = 0.5 * base_ref[r : r + 1, :]
            half_y = 0.5 * base_ref[rows + r : rows + r + 1, :]
            half_depth = 0.5 * base_ref[2 * rows + r : 2 * rows + r + 1, :]
            rotation = base_ref[3 * rows + r : 3 * rows + r + 1, :]
            h, u, v = (field(phase, r, f, c) for f in range(3))
            hx, ux, vx = (across(q, f * rows + r) for f, q in enumerate((h, u, v)))
            hy, uy, vy = (field(phase, r + 1, f, c) - field(phase, r - 1, f, c) for f in range(3))
            state[phase + 1, r, 0, span(c), :] = h - half_x * hx - half_y * hy - half_depth * (ux + vy)
            state[phase + 1, r, 1, span(c), :] = u - half_x * ux - half_y * uy + rotation * v - (0.5 * GRAVITY) * hx
            state[phase + 1, r, 2, span(c), :] = v - half_x * vx - half_y * vy - rotation * u - (0.5 * GRAVITY) * hy

    @pl.when(lat == 0)
    def _():
        above[...] = jnp.zeros(above.shape, jnp.float32)

    @pl.when(lat == lat_n - 1)
    def _():
        below[...] = jnp.zeros(below.shape, jnp.float32)

    for c in range(CHUNKS):
        for r in range(rows):
            for f in range(3):
                p = f * rows + r
                state[0, r, f, span(c), :] = x_ref[pl.ds(c * size * planes + p, size, stride=planes), :]
        pack(0, c)
        send(0, c)

    for c in range(CHUNKS):
        receive(0, c)
        advance(0, c)
        pack(1, c)
        send(1, c)

    for c in range(CHUNKS):
        receive(1, c)
        advance(1, c)
        high = (c + 1) * size
        total = jnp.zeros((size, high), jnp.float32)
        for r in range(rows):
            for f in range(3):
                s_ref[f * rows + r, span(c), :] = state[2, r, f, span(c), :]
                total += dot_t(state[2, r, f, span(c), :], state[2, r, f, 0:high, :])
        gram[span(c), 0:high] = total

    for phase in range(2):
        for c in range(CHUNKS):
            sent(phase, c)

    for c in range(CHUNKS - 1):
        low = (c + 1) * size
        gram[span(c), low:vectors] = gram[low:vectors, span(c)].T

    if not fused:
        gram_ref[...] = gram[...]
        return

    tall = vectors // lon_n
    short = tall // lat_n

    def rs_lon(d):
        return pltpu.make_async_remote_copy(
            src_ref=gram.at[pl.ds(lon_peer(d) * tall, tall), :],
            dst_ref=lon_buf.at[d - 1],
            send_sem=rs_lon_send.at[d - 1], recv_sem=rs_lon_recv.at[d - 1],
            device_id=(lat, lon_peer(d)), device_id_type=MESH,
        )

    def rs_lat(d):
        return pltpu.make_async_remote_copy(
            src_ref=part.at[pl.ds(lat_peer(d) * short, short), :],
            dst_ref=lat_buf.at[d - 1],
            send_sem=rs_lat_send.at[d - 1], recv_sem=rs_lat_recv.at[d - 1],
            device_id=(lat_peer(d), lon), device_id_type=MESH,
        )

    def ag_lat(d):
        return pltpu.make_async_remote_copy(
            src_ref=piece,
            dst_ref=gathered.at[lat],
            send_sem=ag_lat_send.at[d - 1], recv_sem=ag_lat_recv.at[d - 1],
            device_id=(lat_peer(d), lon), device_id_type=MESH,
        )

    def ag_lon(d):
        return pltpu.make_async_remote_copy(
            src_ref=gathered,
            dst_ref=gram_ref.at[lon],
            send_sem=ag_lon_send.at[d - 1], recv_sem=ag_lon_recv.at[d - 1],
            device_id=(lat, lon_peer(d)), device_id_type=MESH,
        )

    def exchange(copy, n):
        for d in range(1, n):
            copy(d).start()
        for d in range(1, n):
            copy(d).wait()

    exchange(rs_lon, lon_n)
    own = gram[pl.ds(lon * tall, tall), :]
    for d in range(lon_n - 1):
        own += lon_buf[d]
    part[...] = own
    exchange(rs_lat, lat_n)
    own = part[pl.ds(lat * short, short), :]
    for d in range(lat_n - 1):
        own += lat_buf[d]
    piece[...] = own
    gathered[lat] = own
    exchange(ag_lat, lat_n)
    gram_ref[lon] = gathered[...]
    exchange(ag_lon, lon_n)


def factor_kernel(cell_total, g_ref, s_ref, out_ref, upper_ref, work, inverse):
    vectors = g_ref.shape[0]
    planes = s_ref.shape[0]
    cells = s_ref.shape[2]
    size = BLOCK
    lane_count = 2 * size if 2 * size >= 128 else 128
    work[:, 0:vectors] = g_ref[...] * (1.0 / cell_total)
    row_i = lax.broadcasted_iota(jnp.int32, (vectors, vectors), 0)
    col_i = lax.broadcasted_iota(jnp.int32, (vectors, vectors), 1)
    work[:, vectors : 2 * vectors] = jnp.where(row_i == col_i, 1.0, 0.0).astype(jnp.float32)
    t_row = lax.broadcasted_iota(jnp.int32, (size, lane_count), 0)
    t_col = lax.broadcasted_iota(jnp.int32, (size, lane_count), 1)
    unit = jnp.where(t_col == t_row + size, 1.0, 0.0).astype(jnp.float32)
    for b in range(vectors // size):
        lo, hi = b * size, (b + 1) * size
        diag = work[lo:hi, lo:hi]
        tile = jnp.concatenate([diag, jnp.zeros((size, lane_count - size), jnp.float32)], axis=1) + unit
        for k in range(size):
            scale = lax.rsqrt(tile[k : k + 1, k : k + 1])
            pivot = tile[k : k + 1, :] * scale
            mult = jnp.where(t_row > k, tile[:, k : k + 1], 0.0) * scale
            tile = jnp.where(t_row == k, pivot, tile - mult * pivot)
        small = tile[:, size : 2 * size]
        panel = dot(small, work[lo:hi, :])
        u = panel[:, 0:vectors]
        upper_ref[lo:hi, :] = jnp.where(col_i[lo:hi, :] >= row_i[lo:hi, :], u, 0.0)
        inverse[lo:hi, :] = panel[:, vectors : 2 * vectors]
        if hi < vectors:
            work[hi:vectors, :] -= t_dot(panel[:, hi:vectors], panel)
    low = inverse[...]
    for p in range(planes):
        out_ref[pl.ds(p, vectors, stride=planes), :] = dot(low, s_ref[p])


def per_device(tangent, base_state):
    lat_n = lax.axis_size("lat")
    lon_n = lax.axis_size("lon")
    vectors, _, rows, cells = tangent.shape
    planes = 3 * rows
    size = vectors // CHUNKS
    fused = vectors % (lon_n * lat_n * 8) == 0
    tall = vectors // lon_n if fused else 8
    short = tall // lat_n if fused else 8
    f32 = jnp.float32
    x = tangent.reshape(vectors * planes, cells)
    base = base_state.reshape(4 * rows, cells)
    vmem = pl.BlockSpec(memory_space=pltpu.VMEM)
    dma = pltpu.SemaphoreType.DMA
    gram_shape = (lon_n, lat_n, short, vectors) if fused else (vectors, vectors)
    stepped, gram = pl.pallas_call(
        functools.partial(step_kernel, lat_n, lon_n, rows, vectors, fused),
        out_shape=(
            jax.ShapeDtypeStruct((planes, vectors, cells), f32),
            jax.ShapeDtypeStruct(gram_shape, f32),
        ),
        in_specs=[vmem, vmem],
        out_specs=(vmem, vmem),
        scratch_shapes=[
            pltpu.VMEM((3, rows, 3, vectors, cells), f32),
            pltpu.VMEM((2, 3, vectors, cells), f32),
            pltpu.VMEM((2, 3, vectors, cells), f32),
            pltpu.VMEM((2, vectors, cells), f32),
            pltpu.VMEM((2, vectors, cells), f32),
            pltpu.VMEM((2, vectors, cells), f32),
            pltpu.VMEM((2, vectors, cells), f32),
            pltpu.VMEM((vectors, vectors), f32),
            pltpu.VMEM((lon_n - 1, tall, vectors), f32),
            pltpu.VMEM((lat_n - 1, short, vectors), f32),
            pltpu.VMEM((tall, vectors), f32),
            pltpu.VMEM((short, vectors), f32),
            pltpu.VMEM((lat_n, short, vectors), f32),
            dma((2, CHUNKS, 2)), dma((2, CHUNKS, 2)), dma((2, CHUNKS, 2)), dma((2, CHUNKS, 2)),
            dma((lon_n - 1,)), dma((lon_n - 1,)), dma((lat_n - 1,)), dma((lat_n - 1,)),
            dma((lat_n - 1,)), dma((lat_n - 1,)), dma((lon_n - 1,)), dma((lon_n - 1,)),
        ],
        compiler_params=pltpu.CompilerParams(
            collective_id=0, has_side_effects=True, vmem_limit_bytes=40 * 2**20
        ),
    )(x, base)
    if fused:
        gram = gram.reshape(vectors, vectors)
    else:
        gram = lax.psum(gram, ("lat", "lon"))
    cell_total = rows * cells * lat_n * lon_n
    out, upper = pl.pallas_call(
        functools.partial(factor_kernel, cell_total),
        out_shape=(
            jax.ShapeDtypeStruct((vectors * planes, cells), f32),
            jax.ShapeDtypeStruct((vectors, vectors), f32),
        ),
        in_specs=[vmem, vmem],
        out_specs=(vmem, vmem),
        scratch_shapes=[
            pltpu.VMEM((vectors, 2 * vectors), f32),
            pltpu.VMEM((vectors, vectors), f32),
        ],
        compiler_params=pltpu.CompilerParams(vmem_limit_bytes=40 * 2**20),
    )(gram, stepped)
    return out.reshape(tangent.shape), upper


def solution(mesh):
    in_specs = (P(None, None, "lat", "lon"), P(None, "lat", "lon"))
    out_specs = (P(None, None, "lat", "lon"), P())
    return jax.shard_map(
        per_device, mesh=mesh, in_specs=in_specs, out_specs=out_specs, check_vma=False
    )
```

time: 291 us -> 107 us (0.37)
  waiting for transfers between devices: 150 us -> 0 us
  Pallas kernels: 0 us -> 104 us
  other arithmetic: 73.4 us -> 0 us
  local copies, waits for them, and re-layouts: 29.4 us -> 2.1 us
  starting transfers between devices: 16.9 us -> 0 us
  between operations: 15.6 us -> 0.65 us
  matrix products: 5.12 us -> 0 us
    psum x1 -> x0, waiting for transfers between devices: 125 us -> none  [per_device(): total = lax.psum(local_gram, ('lat', 'lon'))]
    pallas_call x0 -> x2, Pallas kernels: none -> 104 us  [the longest x1 63.4 us: per_device(): pl.pallas_call(functools.partial(step_kernel, lat_n, lon_n, rows, vectors...]
    another operation x14 -> x0, other arithmetic: 64.3 us -> none  [the longest x6 34.1 us: per_device(): lower_factor = jnp.linalg.cholesky(total / cell_total)]
    ppermute x8 -> x0, waiting for transfers between devices: 25.1 us -> none  [the longest x4 18.1 us: with_halo(): before = lax.ppermute(last, axis, up)]
    ppermute x8 -> x0, starting transfers between devices: 16.8 us -> none  [the longest x4 10.1 us: with_halo(): before = lax.ppermute(last, axis, up)]
    slice x5 -> x0, local copies, waits for them, and re-layouts: 11.1 us -> none  [the longest x4 8.61 us: with_halo(): last = lax.slice_in_dim(shard, length - width, length, axis=dim)]
    ppermute x4 -> x0, local copies, waits for them, and re-layouts: 7.1 us -> none  [the longest x2 4.12 us: with_halo(): before = lax.ppermute(last, axis, up)]
    concatenate x3 -> x0, other arithmetic: 6.41 us -> none  [with_halo(): shard = jnp.concatenate([before, shard, after], axis=dim)]
  transfers between devices with their start and end apart: 9 -> 0, of which waited for: 4 -> 0; matrix products, arithmetic and copies ran while one was open for 6% -> 0% of each run, Pallas kernels for 0% -> 0%
where the time goes in v1:
time: 107 us
  Pallas kernels  104 us (97%)
  local copies, waits for them, and re-layouts  2.1 us (2%)
    pallas_call x1, Pallas kernels, per_device(): pl.pallas_call(functools.partial(step_kernel, lat_n, lon_n, rows, vectors...  63.4 us
    pallas_call x1, Pallas kernels, per_device(): pl.pallas_call(functools.partial(factor_kernel, cell_total), out_shape=(j...  40.9 us

profile of v1, /device:TPU:0, one launch (start us, length us, event | category | flops | bytes accessed | tf_op | source)
XLA Modules:
  0.0 107.0 jit_solution(12473171261009815536)
XLA Ops:
  0.6 0.0 copy-start
  0.6 1.4 %copy-done = f32[256,3,4,128]{3,2,1,0:T(4,128)S(1)} copy-done((f32[256,3,4,128]{3,2,1,0:T(4,128)S(1)}, f32[256,3,4,128]{3,2,1,0:T(4,128)}, u32[]{:S(2)}) %copy-start) | copy-done | bytes 1572888
  2.0 0.0 copy-start.1
  2.0 0.7 copy-done.1
  2.7 63.4 %shard_map.41 = (f32[12,256,128]{2,1,0:T(8,128)S(1)}, f32[4,8,8,256]{3,2,1,0:T(8,128)S(1)}) custom-call(f32[3072,128]{1,0:T(8,128)S(1)} %bitcast.4, f32[16,128]{1,0:T(8,128)S(1)} %bitcast.6), custom_call_target="tpu_custom_call" | custom-call | tf_op jit(solution)/shard_map/pallas_call | solution.py:317
  66.1 40.9 %shard_map.42 = (f32[3072,128]{1,0:T(8,128)}, f32[256,256]{1,0:T(8,128)}) custom-call(f32[256,256]{1,0:T(8,128)S(1)} %bitcast.5, f32[12,256,128]{2,1,0:T(8,128)S(1)} %get-tuple-element.7.s_ref), custom_call_target="tpu_custom_call" | custom-call | tf_op jit(solution)/shard_map/pallas_call | solution.py:352
Async XLA Ops:
  0.6 1.4 %copy-start = (f32[256,3,4,128]{3,2,1,0:T(4,128)S(1)}, f32[256,3,4,128]{3,2,1,0:T(4,128)}, u32[]{:S(2)}) copy-start(f32[256,3,4,128]{3,2,1,0:T(4,128)} %param.2) | copy-start | bytes 4718596
  2.0 0.7 copy-start.1

commit v2 on v1

--- a/solution.py
+++ b/solution.py
@@ -263,6 +263,61 @@
     exchange(ag_lat, lat_n)
     gram_ref[lon] = gathered[...]
     exchange(ag_lon, lon_n)
+
+
+def eliminate(tile, size):
+    lanes = tile.shape[1]
+    row = lax.broadcasted_iota(jnp.int32, (8, lanes), 0)
+
+    def lane(q, k):
+        return jnp.broadcast_to(q[:, k : k + 1], (8, lanes))
+
+    def sub(q, k):
+        return jnp.broadcast_to(q[k : k + 1, :], (8, lanes))
+
+    groups = [tile[8 * g : 8 * g + 8, :] for g in range(size // 8)]
+    for g in range(size // 8):
+        cols = [lane(groups[g], 8 * g + j) for j in range(8)]
+        below = [[lane(groups[m], 8 * g + j) for j in range(8)] for m in range(g + 1, size // 8)]
+        rows = [sub(groups[g], j) for j in range(8)]
+        a = {(i, j): sub(cols[j], i) for j in range(8) for i in range(j, 8)}
+        scale = []
+        for k in range(8):
+            scale.append(lax.rsqrt(a[k, k]))
+            for i in range(k + 1, 8):
+                a[i, k] = a[i, k] * scale[k]
+            for j in range(k + 1, 8):
+                for i in range(j, 8):
+                    a[i, j] = a[i, j] - a[i, k] * a[j, k]
+        w = {}
+        for i in range(8):
+            w[i, i] = scale[i]
+            for j in range(i):
+                acc = a[i, j] * w[j, j]
+                for m in range(j + 1, i):
+                    acc = acc + a[i, m] * w[m, j]
+                w[i, j] = -acc * scale[i]
+        new = None
+        for j in range(8):
+            column = jnp.zeros((8, lanes), jnp.float32)
+            for i in range(j, 8):
+                column = jnp.where(row == i, w[i, j], column)
+            term = column * rows[j]
+            new = term if new is None else new + term
+        groups[g] = new
+        if g + 1 < size // 8:
+            pivots = [sub(new, j) for j in range(8)]
+            for n, m in enumerate(range(g + 1, size // 8)):
+                change = None
+                for j in range(8):
+                    mult = None
+                    for k in range(j + 1):
+                        t = w[j, k] * below[n][k]
+                        mult = t if mult is None else mult + t
+                    t = mult * pivots[j]
+                    change = t if change is None else change + t
+                groups[m] = groups[m] - change
+    return jnp.concatenate(groups, axis=0)
 
 
 def factor_kernel(cell_total, g_ref, s_ref, out_ref, upper_ref, work, inverse):
@@ -282,11 +337,7 @@
         lo, hi = b * size, (b + 1) * size
         diag = work[lo:hi, lo:hi]
         tile = jnp.concatenate([diag, jnp.zeros((size, lane_count - size), jnp.float32)], axis=1) + unit
-        for k in range(size):
-            scale = lax.rsqrt(tile[k : k + 1, k : k + 1])
-            pivot = tile[k : k + 1, :] * scale
-            mult = jnp.where(t_row > k, tile[:, k : k + 1], 0.0) * scale
-            tile = jnp.where(t_row == k, pivot, tile - mult * pivot)
+        tile = eliminate(tile, size)
         small = tile[:, size : 2 * size]
         panel = dot(small, work[lo:hi, :])
         u = panel[:, 0:vectors]

time: 107 us -> 83.2 us (0.78)
  Pallas kernels: 104 us -> 80.2 us
    pallas_call x1, Pallas kernels: 40.9 us -> 16.8 us  [per_device(): pl.pallas_call(functools.partial(factor_kernel, cell_total), out_shape=(j...]
where the time goes in v2:
time: 83.2 us; the launch traced here: 82.9 us
  Pallas kernels  80.2 us (96%)
  local copies, waits for them, and re-layouts  2.1 us (3%)
    pallas_call x1, Pallas kernels, per_device(): pl.pallas_call(functools.partial(step_kernel, lat_n, lon_n, rows, vectors...  63.4 us
    pallas_call x1, Pallas kernels, per_device(): pl.pallas_call(functools.partial(factor_kernel, cell_total), out_shape=(j...  16.8 us
    unnamed x4, local copies, waits for them, and re-layouts  2.1 us

profile of v2, /device:TPU:0, one launch (start us, length us, event | category | flops | bytes accessed | tf_op | source)
XLA Modules:
  0.0 82.9 jit_solution(3380068375104000720)
XLA Ops:
  0.6 0.0 copy-start
  0.6 1.4 %copy-done = f32[256,3,4,128]{3,2,1,0:T(4,128)S(1)} copy-done((f32[256,3,4,128]{3,2,1,0:T(4,128)S(1)}, f32[256,3,4,128]{3,2,1,0:T(4,128)}, u32[]{:S(2)}) %copy-start) | copy-done | bytes 1572888
  2.0 0.0 copy-start.1
  2.0 0.7 copy-done.1
  2.7 63.4 %shard_map.41 = (f32[12,256,128]{2,1,0:T(8,128)S(1)}, f32[4,8,8,256]{3,2,1,0:T(8,128)S(1)}) custom-call(f32[3072,128]{1,0:T(8,128)S(1)} %bitcast.4, f32[16,128]{1,0:T(8,128)S(1)} %bitcast.6), custom_call_target="tpu_custom_call" | custom-call | tf_op jit(solution)/shard_map/pallas_call | solution.py:368
  66.1 16.8 %shard_map.42 = (f32[3072,128]{1,0:T(8,128)}, f32[256,256]{1,0:T(8,128)}) custom-call(f32[256,256]{1,0:T(8,128)S(1)} %bitcast.5, f32[12,256,128]{2,1,0:T(8,128)S(1)} %get-tuple-element.7.s_ref), custom_call_target="tpu_custom_call" | custom-call | tf_op jit(solution)/shard_map/pallas_call | solution.py:403
Async XLA Ops:
  0.6 1.4 %copy-start = (f32[256,3,4,128]{3,2,1,0:T(4,128)S(1)}, f32[256,3,4,128]{3,2,1,0:T(4,128)}, u32[]{:S(2)}) copy-start(f32[256,3,4,128]{3,2,1,0:T(4,128)} %param.2) | copy-start | bytes 4718596
  2.0 0.7 copy-start.1

commit v3 on v2

--- a/solution.py
+++ b/solution.py
@@ -31,12 +31,11 @@
 
 
 def step_kernel(
-    lat_n, lon_n, rows, vectors, fused, x_ref, base_ref, s_ref, gram_ref,
+    lat_n, lon_n, rows, vectors, fused, x_ref, base_ref, s_ref, first_ref, second_ref,
     state, above, below, to_west, to_east, from_west, from_east,
-    gram, lon_buf, lat_buf, part, piece, gathered,
+    gram, lon_buf, lat_buf, whole,
     row_send, row_recv, col_send, col_recv,
-    rs_lon_send, rs_lon_recv, rs_lat_send, rs_lat_recv,
-    ag_lat_send, ag_lat_recv, ag_lon_send, ag_lon_recv,
+    rs_send, rs_recv, lat_send, lat_recv, ag_send, ag_recv,
 ):
     lat = lax.axis_index("lat")
     lon = lax.axis_index("lon")
@@ -185,84 +184,135 @@
         pack(1, c)
         send(1, c)
 
+    def gram_rows(c):
+        high = (c + 1) * size
+        mine, all_so_far = [], []
+        for r in range(rows):
+            for f in range(3):
+                q = state[2, r, f, span(c), :]
+                s_ref[f * rows + r, span(c), :] = q
+                mine.append(q)
+                all_so_far.append(state[2, r, f, 0:high, :])
+        gram[span(c), 0:high] = dot_t(
+            jnp.concatenate(mine, axis=1), jnp.concatenate(all_so_far, axis=1)
+        )
+
+    def halos_sent():
+        for phase in range(2):
+            for c in range(CHUNKS):
+                sent(phase, c)
+
+    if not fused:
+        for c in range(CHUNKS):
+            receive(1, c)
+            advance(1, c)
+            gram_rows(c)
+        halos_sent()
+        for c in range(CHUNKS - 1):
+            low = (c + 1) * size
+            gram[span(c), low:vectors] = gram[low:vectors, span(c)].T
+        first_ref[...] = gram[...]
+        second_ref[...] = jnp.zeros(second_ref.shape, jnp.float32)
+        return
+
+    inv_ref, low_ref = first_ref, second_ref
+    short = size // lon_n
+    scale = 1.0 / (rows * cells * lat_n * lon_n)
+
+    def wide(c):
+        return -(-((c + 1) * size) // 128) * 128
+
+    def rs(c, d):
+        return pltpu.make_async_remote_copy(
+            src_ref=gram.at[pl.ds(c * size + lon_peer(d) * short, short), 0 : wide(c)],
+            dst_ref=lon_buf.at[c, d - 1, :, 0 : wide(c)],
+            send_sem=rs_send.at[c, d - 1], recv_sem=rs_recv.at[c, d - 1],
+            device_id=(lat, lon_peer(d)), device_id_type=MESH,
+        )
+
+    def over_lat(c, d):
+        return pltpu.make_async_remote_copy(
+            src_ref=lat_buf.at[c, lat, :, 0 : wide(c)],
+            dst_ref=lat_buf.at[c, lat, :, 0 : wide(c)],
+            send_sem=lat_send.at[c, d - 1], recv_sem=lat_recv.at[c, d - 1],
+            device_id=(lat_peer(d), lon), device_id_type=MESH,
+        )
+
+    def ag(c, d):
+        return pltpu.make_async_remote_copy(
+            src_ref=whole.at[c, lon, :, 0 : wide(c)],
+            dst_ref=whole.at[c, lon, :, 0 : wide(c)],
+            send_sem=ag_send.at[c, d - 1], recv_sem=ag_recv.at[c, d - 1],
+            device_id=(lat, lon_peer(d)), device_id_type=MESH,
+        )
+
+    def scatter(c):
+        for d in range(1, lon_n):
+            rs(c, d).start()
+
+    def across_lat(c):
+        for d in range(1, lon_n):
+            rs(c, d).wait()
+        own = gram[pl.ds(c * size + lon * short, short), 0 : wide(c)]
+        for d in range(lon_n - 1):
+            own += lon_buf[c, d, :, 0 : wide(c)]
+        lat_buf[c, lat, :, 0 : wide(c)] = own
+        for d in range(1, lat_n):
+            over_lat(c, d).start()
+
+    def gather(c):
+        for d in range(1, lat_n):
+            over_lat(c, d).wait()
+        total = lat_buf[c, 0, :, 0 : wide(c)]
+        for i in range(1, lat_n):
+            total += lat_buf[c, i, :, 0 : wide(c)]
+        whole[c, lon, :, 0 : wide(c)] = total * scale
+        for d in range(1, lon_n):
+            ag(c, d).start()
+
+    t_row = lax.broadcasted_iota(jnp.int32, (size, 2 * size), 0)
+    t_col = lax.broadcasted_iota(jnp.int32, (size, 2 * size), 1)
+    unit = jnp.where(t_col == t_row + size, 1.0, 0.0).astype(jnp.float32)
+    inv_ref[...] = jnp.zeros(inv_ref.shape, jnp.float32)
+    low_ref[...] = jnp.zeros(low_ref.shape, jnp.float32)
+    gram[...] = jnp.zeros(gram.shape, jnp.float32)
+
+    def factor(c):
+        for d in range(1, lon_n):
+            ag(c, d).wait()
+        lo, hi = c * size, (c + 1) * size
+        mine = whole[c, :, :, 0 : wide(c)].reshape(size, wide(c))
+        diag = mine[:, lo:hi]
+        if c:
+            done = inv_ref[0:lo, 0:lo]
+            left = dot_t(mine[:, 0:lo], done)
+            diag = diag - dot_t(left, left)
+            low_ref[lo:hi, 0:lo] = left
+            carry = dot(left, done)
+        tile = eliminate(jnp.concatenate([diag, jnp.zeros_like(diag)], axis=1) + unit, size)
+        small = tile[:, size : 2 * size]
+        inv_ref[lo:hi, lo:hi] = small
+        low_ref[lo:hi, lo:hi] = tile[:, 0:size].T
+        if c:
+            inv_ref[lo:hi, 0:lo] = -dot(small, carry)
+
+    last = CHUNKS - 1
     for c in range(CHUNKS):
         receive(1, c)
         advance(1, c)
-        high = (c + 1) * size
-        total = jnp.zeros((size, high), jnp.float32)
-        for r in range(rows):
-            for f in range(3):
-                s_ref[f * rows + r, span(c), :] = state[2, r, f, span(c), :]
-                total += dot_t(state[2, r, f, span(c), :], state[2, r, f, 0:high, :])
-        gram[span(c), 0:high] = total
-
-    for phase in range(2):
-        for c in range(CHUNKS):
-            sent(phase, c)
-
-    for c in range(CHUNKS - 1):
-        low = (c + 1) * size
-        gram[span(c), low:vectors] = gram[low:vectors, span(c)].T
-
-    if not fused:
-        gram_ref[...] = gram[...]
-        return
-
-    tall = vectors // lon_n
-    short = tall // lat_n
-
-    def rs_lon(d):
-        return pltpu.make_async_remote_copy(
-            src_ref=gram.at[pl.ds(lon_peer(d) * tall, tall), :],
-            dst_ref=lon_buf.at[d - 1],
-            send_sem=rs_lon_send.at[d - 1], recv_sem=rs_lon_recv.at[d - 1],
-            device_id=(lat, lon_peer(d)), device_id_type=MESH,
-        )
-
-    def rs_lat(d):
-        return pltpu.make_async_remote_copy(
-            src_ref=part.at[pl.ds(lat_peer(d) * short, short), :],
-            dst_ref=lat_buf.at[d - 1],
-            send_sem=rs_lat_send.at[d - 1], recv_sem=rs_lat_recv.at[d - 1],
-            device_id=(lat_peer(d), lon), device_id_type=MESH,
-        )
-
-    def ag_lat(d):
-        return pltpu.make_async_remote_copy(
-            src_ref=piece,
-            dst_ref=gathered.at[lat],
-            send_sem=ag_lat_send.at[d - 1], recv_sem=ag_lat_recv.at[d - 1],
-            device_id=(lat_peer(d), lon), device_id_type=MESH,
-        )
-
-    def ag_lon(d):
-        return pltpu.make_async_remote_copy(
-            src_ref=gathered,
-            dst_ref=gram_ref.at[lon],
-            send_sem=ag_lon_send.at[d - 1], recv_sem=ag_lon_recv.at[d - 1],
-            device_id=(lat, lon_peer(d)), device_id_type=MESH,
-        )
-
-    def exchange(copy, n):
-        for d in range(1, n):
-            copy(d).start()
-        for d in range(1, n):
-            copy(d).wait()
-
-    exchange(rs_lon, lon_n)
-    own = gram[pl.ds(lon * tall, tall), :]
-    for d in range(lon_n - 1):
-        own += lon_buf[d]
-    part[...] = own
-    exchange(rs_lat, lat_n)
-    own = part[pl.ds(lat * short, short), :]
-    for d in range(lat_n - 1):
-        own += lat_buf[d]
-    piece[...] = own
-    gathered[lat] = own
-    exchange(ag_lat, lat_n)
-    gram_ref[lon] = gathered[...]
-    exchange(ag_lon, lon_n)
+        gram_rows(c)
+        scatter(c)
+        if c >= 1:
+            gather(c - 1)
+        if c < last:
+            across_lat(c)
+        if c >= 2:
+            factor(c - 2)
+    across_lat(last)
+    factor(last - 1)
+    gather(last)
+    factor(last)
+    halos_sent()
 
 
 def eliminate(tile, size):
@@ -350,29 +400,40 @@
         out_ref[pl.ds(p, vectors, stride=planes), :] = dot(low, s_ref[p])
 
 
+def solve_kernel(inv_ref, low_ref, s_ref, out_ref, upper_ref):
+    vectors = inv_ref.shape[0]
+    planes = s_ref.shape[0]
+    cells = s_ref.shape[2]
+    row_i = lax.broadcasted_iota(jnp.int32, (vectors, vectors), 0)
+    col_i = lax.broadcasted_iota(jnp.int32, (vectors, vectors), 1)
+    upper_ref[...] = jnp.where(col_i >= row_i, low_ref[...].T, 0.0)
+    low = inv_ref[...]
+    for p in range(0, planes, 2):
+        both = dot(low, jnp.concatenate([s_ref[p], s_ref[p + 1]], axis=1))
+        out_ref[pl.ds(p, vectors, stride=planes), :] = both[:, 0:cells]
+        out_ref[pl.ds(p + 1, vectors, stride=planes), :] = both[:, cells : 2 * cells]
+
+
 def per_device(tangent, base_state):
     lat_n = lax.axis_size("lat")
     lon_n = lax.axis_size("lon")
     vectors, _, rows, cells = tangent.shape
     planes = 3 * rows
     size = vectors // CHUNKS
-    fused = vectors % (lon_n * lat_n * 8) == 0
-    tall = vectors // lon_n if fused else 8
-    short = tall // lat_n if fused else 8
+    fused = size % (lon_n * 8) == 0
+    short = size // lon_n if fused else 8
     f32 = jnp.float32
     x = tangent.reshape(vectors * planes, cells)
     base = base_state.reshape(4 * rows, cells)
     vmem = pl.BlockSpec(memory_space=pltpu.VMEM)
     dma = pltpu.SemaphoreType.DMA
-    gram_shape = (lon_n, lat_n, short, vectors) if fused else (vectors, vectors)
-    stepped, gram = pl.pallas_call(
+    square = jax.ShapeDtypeStruct((vectors, vectors), f32)
+    flat = jax.ShapeDtypeStruct((vectors * planes, cells), f32)
+    stepped, first, second = pl.pallas_call(
         functools.partial(step_kernel, lat_n, lon_n, rows, vectors, fused),
-        out_shape=(
-            jax.ShapeDtypeStruct((planes, vectors, cells), f32),
-            jax.ShapeDtypeStruct(gram_shape, f32),
-        ),
+        out_shape=(jax.ShapeDtypeStruct((planes, vectors, cells), f32), square, square),
         in_specs=[vmem, vmem],
-        out_specs=(vmem, vmem),
+        out_specs=(vmem, vmem, vmem),
         scratch_shapes=[
             pltpu.VMEM((3, rows, 3, vectors, cells), f32),
             pltpu.VMEM((2, 3, vectors, cells), f32),
@@ -382,38 +443,41 @@
             pltpu.VMEM((2, vectors, cells), f32),
             pltpu.VMEM((2, vectors, cells), f32),
             pltpu.VMEM((vectors, vectors), f32),
-            pltpu.VMEM((lon_n - 1, tall, vectors), f32),
-            pltpu.VMEM((lat_n - 1, short, vectors), f32),
-            pltpu.VMEM((tall, vectors), f32),
-            pltpu.VMEM((short, vectors), f32),
-            pltpu.VMEM((lat_n, short, vectors), f32),
+            pltpu.VMEM((CHUNKS, lon_n - 1, short, vectors), f32),
+            pltpu.VMEM((CHUNKS, lat_n, short, vectors), f32),
+            pltpu.VMEM((CHUNKS, lon_n, short, vectors), f32),
             dma((2, CHUNKS, 2)), dma((2, CHUNKS, 2)), dma((2, CHUNKS, 2)), dma((2, CHUNKS, 2)),
-            dma((lon_n - 1,)), dma((lon_n - 1,)), dma((lat_n - 1,)), dma((lat_n - 1,)),
-            dma((lat_n - 1,)), dma((lat_n - 1,)), dma((lon_n - 1,)), dma((lon_n - 1,)),
+            dma((CHUNKS, lon_n - 1)), dma((CHUNKS, lon_n - 1)),
+            dma((CHUNKS, lat_n - 1)), dma((CHUNKS, lat_n - 1)),
+            dma((CHUNKS, lon_n - 1)), dma((CHUNKS, lon_n - 1)),
         ],
         compiler_params=pltpu.CompilerParams(
             collective_id=0, has_side_effects=True, vmem_limit_bytes=40 * 2**20
         ),
     )(x, base)
+    local = pltpu.CompilerParams(vmem_limit_bytes=40 * 2**20)
     if fused:
-        gram = gram.reshape(vectors, vectors)
+        out, upper = pl.pallas_call(
+            solve_kernel,
+            out_shape=(flat, square),
+            in_specs=[vmem, vmem, vmem],
+            out_specs=(vmem, vmem),
+            compiler_params=local,
+        )(first, second, stepped)
     else:
-        gram = lax.psum(gram, ("lat", "lon"))
-    cell_total = rows * cells * lat_n * lon_n
-    out, upper = pl.pallas_call(
-        functools.partial(factor_kernel, cell_total),
-        out_shape=(
-            jax.ShapeDtypeStruct((vectors * planes, cells), f32),
-            jax.ShapeDtypeStruct((vectors, vectors), f32),
-        ),
-        in_specs=[vmem, vmem],
-        out_specs=(vmem, vmem),
-        scratch_shapes=[
-            pltpu.VMEM((vectors, 2 * vectors), f32),
-            pltpu.VMEM((vectors, vectors), f32),
-        ],
-        compiler_params=pltpu.CompilerParams(vmem_limit_bytes=40 * 2**20),
-    )(gram, stepped)
+        total = lax.psum(first, ("lat", "lon"))
+        cell_total = rows * cells * lat_n * lon_n
+        out, upper = pl.pallas_call(
+            functools.partial(factor_kernel, cell_total),
+            out_shape=(flat, square),
+            in_specs=[vmem, vmem],
+            out_specs=(vmem, vmem),
+            scratch_shapes=[
+                pltpu.VMEM((vectors, 2 * vectors), f32),
+                pltpu.VMEM((vectors, vectors), f32),
+            ],
+            compiler_params=local,
+        )(total, stepped)
     return out.reshape(tangent.shape), upper
 
 

time: 83.2 us -> 74.1 us (0.89)
  Pallas kernels: 80.2 us -> 71.1 us
    pallas_call x1, Pallas kernels: 16.8 us -> 2.63 us  [per_device(): pl.pallas_call(solve_kernel, out_shape=(flat, square), in_specs=[vmem, vm...]
    pallas_call x1, Pallas kernels: 63.4 us -> 68.5 us  [per_device(): pl.pallas_call(functools.partial(step_kernel, lat_n, lon_n, rows, vectors...]
where the time goes in v3:
time: 74.1 us; the launch traced here: 73.9 us
  Pallas kernels  71.1 us (96%)
  local copies, waits for them, and re-layouts  2.1 us (3%)
    pallas_call x1, Pallas kernels, per_device(): pl.pallas_call(functools.partial(step_kernel, lat_n, lon_n, rows, vectors...  68.5 us
    pallas_call x1, Pallas kernels, per_device(): pl.pallas_call(solve_kernel, out_shape=(flat, square), in_specs=[vmem, vm...  2.63 us
    unnamed x4, local copies, waits for them, and re-layouts  2.1 us

profile of v3, /device:TPU:0, one launch (start us, length us, event | category | flops | bytes accessed | tf_op | source)
XLA Modules:
  0.0 73.9 jit_solution(6006548645223246828)
XLA Ops:
  0.6 0.0 copy-start
  0.6 1.4 %copy-done = f32[256,3,4,128]{3,2,1,0:T(4,128)S(1)} copy-done((f32[256,3,4,128]{3,2,1,0:T(4,128)S(1)}, f32[256,3,4,128]{3,2,1,0:T(4,128)}, u32[]{:S(2)}) %copy-start) | copy-done | bytes 1572888
  2.0 0.0 copy-start.1
  2.0 0.7 copy-done.1
  2.7 68.5 %shard_map.41 = (f32[12,256,128]{2,1,0:T(8,128)S(1)}, f32[256,256]{1,0:T(8,128)S(1)}, f32[256,256]{1,0:T(8,128)S(1)}) custom-call(f32[3072,128]{1,0:T(8,128)S(1)} %bitcast.3, f32[16,128]{1,0:T(8,128)S(1)} %bitcast.4), custom_call_target="tpu_custom_call" | custom-call | tf_op jit(solution)/shard_map/pallas_call | solution.py:432
  71.2 2.6 %shard_map.42 = (f32[3072,128]{1,0:T(8,128)}, f32[256,256]{1,0:T(8,128)}) custom-call(f32[256,256]{1,0:T(8,128)S(1)} %get-tuple-element.7.inv_ref, f32[256,256]{1,0:T(8,128)S(1)} %get-tuple-element.8.low_ref, f32[12,256,128]{2,1,0:T(8,128)S(1)} %get-tuple-element.9.s_ref), custom_call_target="tpu_custom_call" | custom-call | tf_op jit(solution)/shard_map/pallas_call | solution.py:460
Async XLA Ops:
  0.6 1.4 %copy-start = (f32[256,3,4,128]{3,2,1,0:T(4,128)S(1)}, f32[256,3,4,128]{3,2,1,0:T(4,128)}, u32[]{:S(2)}) copy-start(f32[256,3,4,128]{3,2,1,0:T(4,128)} %param.2) | copy-start | bytes 4718596
  2.0 0.7 copy-start.1

commit v4 on v3

--- a/solution.py
+++ b/solution.py
@@ -170,7 +170,7 @@
     def _():
         below[...] = jnp.zeros(below.shape, jnp.float32)
 
-    for c in range(CHUNKS):
+    def begin(c):
         for r in range(rows):
             for f in range(3):
                 p = f * rows + r
@@ -178,11 +178,27 @@
         pack(0, c)
         send(0, c)
 
-    for c in range(CHUNKS):
+    def middle(c):
         receive(0, c)
         advance(0, c)
         pack(1, c)
         send(1, c)
+
+    def halos(c):
+        if c == 0:
+            begin(0)
+            begin(1)
+            sent(0, 0)
+            begin(2)
+            middle(0)
+            sent(0, 1)
+            for n in range(3, CHUNKS):
+                begin(n)
+            middle(1)
+        if c + 2 < CHUNKS:
+            middle(c + 2)
+        receive(1, c)
+        advance(1, c)
 
     def gram_rows(c):
         high = (c + 1) * size
@@ -198,14 +214,14 @@
         )
 
     def halos_sent():
-        for phase in range(2):
-            for c in range(CHUNKS):
-                sent(phase, c)
+        for c in range(2, CHUNKS):
+            sent(0, c)
+        for c in range(CHUNKS):
+            sent(1, c)
 
     if not fused:
         for c in range(CHUNKS):
-            receive(1, c)
-            advance(1, c)
+            halos(c)
             gram_rows(c)
         halos_sent()
         for c in range(CHUNKS - 1):
@@ -298,8 +314,7 @@
 
     last = CHUNKS - 1
     for c in range(CHUNKS):
-        receive(1, c)
-        advance(1, c)
+        halos(c)
         gram_rows(c)
         scatter(c)
         if c >= 1:

time: 74.1 us -> 70.4 us (0.950)
  Pallas kernels: 71.1 us -> 67.4 us
    pallas_call x1, Pallas kernels: 68.5 us -> 64.8 us  [per_device(): pl.pallas_call(functools.partial(step_kernel, lat_n, lon_n, rows, vectors...]
where the time goes in v4:
time: 70.4 us; the launch traced here: 70.1 us
  Pallas kernels  67.4 us (96%)
  local copies, waits for them, and re-layouts  2.1 us (3%)
    pallas_call x1, Pallas kernels, per_device(): pl.pallas_call(functools.partial(step_kernel, lat_n, lon_n, rows, vectors...  64.8 us
    pallas_call x1, Pallas kernels, per_device(): pl.pallas_call(solve_kernel, out_shape=(flat, square), in_specs=[vmem, vm...  2.63 us
    unnamed x4, local copies, waits for them, and re-layouts  2.1 us

profile of v4, /device:TPU:0, one launch (start us, length us, event | category | flops | bytes accessed | tf_op | source)
XLA Modules:
  0.0 70.1 jit_solution(12681084173837169790)
XLA Ops:
  0.6 0.0 copy-start
  0.6 1.4 %copy-done = f32[256,3,4,128]{3,2,1,0:T(4,128)S(1)} copy-done((f32[256,3,4,128]{3,2,1,0:T(4,128)S(1)}, f32[256,3,4,128]{3,2,1,0:T(4,128)}, u32[]{:S(2)}) %copy-start) | copy-done | bytes 1572888
  2.0 0.0 copy-start.1
  2.0 0.7 copy-done.1
  2.7 64.8 %shard_map.41 = (f32[12,256,128]{2,1,0:T(8,128)S(1)}, f32[256,256]{1,0:T(8,128)S(1)}, f32[256,256]{1,0:T(8,128)S(1)}) custom-call(f32[3072,128]{1,0:T(8,128)S(1)} %bitcast.3, f32[16,128]{1,0:T(8,128)S(1)} %bitcast.4), custom_call_target="tpu_custom_call" | custom-call | tf_op jit(solution)/shard_map/pallas_call | solution.py:447
  67.5 2.6 %shard_map.42 = (f32[3072,128]{1,0:T(8,128)}, f32[256,256]{1,0:T(8,128)}) custom-call(f32[256,256]{1,0:T(8,128)S(1)} %get-tuple-element.7.inv_ref, f32[256,256]{1,0:T(8,128)S(1)} %get-tuple-element.8.low_ref, f32[12,256,128]{2,1,0:T(8,128)S(1)} %get-tuple-element.9.s_ref), custom_call_target="tpu_custom_call" | custom-call | tf_op jit(solution)/shard_map/pallas_call | solution.py:475
Async XLA Ops:
  0.6 1.4 %copy-start = (f32[256,3,4,128]{3,2,1,0:T(4,128)S(1)}, f32[256,3,4,128]{3,2,1,0:T(4,128)}, u32[]{:S(2)}) copy-start(f32[256,3,4,128]{3,2,1,0:T(4,128)} %param.2) | copy-start | bytes 4718596
  2.0 0.7 copy-start.1
